TPU v7x, 512 devices: a whole 4x4x16 slice. The times are simulated.
512 devices in a mesh: section: 16 (over z), seq: 32 (over y, x, core).
Axes of the slice: x: 4, y: 4, z: 16, core: 2. Of those that a mesh axis runs over, the one named last changes fastest.
Arguments:
- fresh: bfloat16 [16, 512, 3, 4096], P('section', 'seq'), may hold values from -16 to 16
- stale: bfloat16 [16, 16, 512, 2, 4096], P('section', None, None, None, 'seq'), may hold values from -6 to 6
- section_patch: int32 [16], P('section'), may hold values from 0 to 15, as said below
Outputs:
- handed: bfloat16 [16, 512, 4096], P('section', 'seq')
Inputs may be any that keep to these rules, and one draw needn't show every extreme that they name: section_patch[s] = (t - s) mod 16 for a plan offset t, so each patch is at exactly one section.
All inputs are finite; a program needn't handle non-finite values.
Results may differ from a plain program's by a relative error of at most 0.0048.
Values may be sent and summed in bfloat16 or wider, within the bound.
No kernel may reach another device: no remote copies, remote signals or barrier semaphores. Data moves between devices by JAX's collectives and lax.ppermute only.
A program may use at most 128 MiB of HBM per device.

v0:
```python
import math

import jax
import jax.numpy as jnp
from jax import lax
from jax.sharding import PartitionSpec as P

HD = 128


def shifted(value, axis, steps):
    count = lax.axis_size(axis)
    pairs = [(source, (source + steps) % count) for source in range(count)]
    return lax.ppermute(value, axis, pairs)


def combine(new_scores, old_scores, new_values, old_values):
    top = jnp.maximum(
        jnp.max(new_scores, axis=-1, keepdims=True), jnp.max(old_scores, axis=-1, keepdims=True)
    )
    new_expo = jnp.exp(new_scores - top)
    old_expo = jnp.exp(old_scores - top)
    total = jnp.sum(new_expo, axis=-1, keepdims=True) + jnp.sum(old_expo, axis=-1, keepdims=True)
    summed = jnp.dot(new_expo.astype(jnp.bfloat16), new_values, preferred_element_type=jnp.float32)
    summed = summed + jnp.dot(
        old_expo.astype(jnp.bfloat16), old_values, preferred_element_type=jnp.float32
    )
    return (summed / total).astype(jnp.bfloat16)


def body(fresh, stale, section_patch):
    own = section_patch[0]
    count = stale.shape[1]
    patch_len = stale.shape[2]
    width = stale.shape[-1]
    head_size = HD
    scale = head_size ** (-0.5)
    cache = stale[0].reshape(count * patch_len, 2 * width)
    slot_ids = jnp.arange(count * patch_len, dtype=jnp.int32) // patch_len
    hidden_slot = (slot_ids == own)[None, :]

    def stale_scores(qrows, head):
        keys = cache[:, head * head_size : (head + 1) * head_size]
        scores = (
            lax.dot_general(
                qrows, keys, (((1,), (1,)), ((), ())), preferred_element_type=jnp.float32
            )
            * scale
        )
        return jnp.where(hidden_slot, -1e30, scores)

    def fresh_scores(qrows, new_keys):
        return (
            lax.dot_general(
                qrows, new_keys, (((1,), (1,)), ((), ())), preferred_element_type=jnp.float32
            )
            * scale
        )

    local = lax.all_to_all(fresh, "seq", split_axis=3, concat_axis=1, tiled=True)[0]
    length = local.shape[0]
    flat = local.reshape(length, 3 * width)
    block = math.gcd(length, 256)
    head = 0
    low = head * head_size
    queries = flat[:, low : low + head_size]
    new_keys = flat[:, width + low : width + low + head_size]
    new_values = flat[:, 2 * width + low : 2 * width + low + head_size]
    old_values = cache[:, width + low : width + low + head_size]
    blocks = queries.reshape(length // block, block, head_size)

    def one_block(qrows):
        return combine(
            fresh_scores(qrows, new_keys), stale_scores(qrows, head), new_values, old_values
        )

    outputs = lax.map(one_block, blocks).reshape(length, head_size)
    attended = outputs
    attended = attended.reshape(1, length, width)
    back = lax.all_to_all(attended, "seq", split_axis=1, concat_axis=2, tiled=True)
    return shifted(back, "section", 1)


def solution(mesh):
    return jax.shard_map(
        body,
        mesh=mesh,
        in_specs=(
            P("section", "seq", None, None),
            P("section", None, None, None, "seq"),
            P("section"),
        ),
        out_specs=P("section", "seq", None),
        check_vma=False,
    )
```

profile of v0, /device:TPU:1, one launch (start us, length us, event | category | flops | bytes accessed | tf_op | source)
XLA Modules:
  0.0 88.1 jit_solution(11627659992674859169)
XLA Ops:
  0.0 5.7 %copy.11 = bf16[1,16,3,4096]{1,2,0,3:T(4,128)(2,1)} copy(bf16[1,16,3,4096]{3,1,2,0:T(8,128)(2,1)} %param.5) | data formatting | bytes 786432 | tf_op args[0]
  5.7 7.5 %reshape.55 = bf16[32,2,3072]{2,1,0:T(2,128)(2,1)} reshape(bf16[4096,1,3,16]{3,2,1,0:T(4,128)(2,1)} %bitcast.59) | data formatting | bytes 786432
  13.2 10.4 %all-to-all-start = ((bf16[32,2,3072]{2,1,0:T(2,128)(2,1)}), bf16[32,2,3072]{2,1,0:T(2,128)(2,1)S(1)}, u32[]{:S(2)}, u32[]{:S(2)}) async-start(bf16[32,2,3072]{2,1,0:T(2,128)(2,1)} %reshape.55), calls=%async_computation | async-start | bytes 786432 | tf_op jit(solution)/shard_map/all_to_all | solution.py:60
  23.6 2.7 %copy.23 = bf16[1024,8,2,128]{3,1,2,0:T(8,128)(2,1)S(1)} copy(bf16[1024,8,2,128]{3,2,1,0:T(2,128)(2,1)} %bitcast.61) | data formatting | bytes 8388608
  26.4 1.9 %copy-done = bf16[1024,8,2,128]{3,1,2,0:T(8,128)(2,1)} copy-done((bf16[1024,8,2,128]{3,1,2,0:T(8,128)(2,1)}, bf16[1024,8,2,128]{3,1,2,0:T(8,128)(2,1)S(1)}, u32[]{:S(2)}) %copy-start) | copy-done | bytes 4194328
  28.4 5.5 %all-to-all-done = bf16[32,2,3072]{2,1,0:T(2,128)(2,1)S(1)} async-done(((bf16[32,2,3072]{2,1,0:T(2,128)(2,1)}), bf16[32,2,3072]{2,1,0:T(2,128)(2,1)S(1)}, u32[]{:S(2)}, u32[]{:S(2)}) %all-to-all-start) | async-done | bytes 393248 | tf_op jit(solution)/shard_map/all_to_all | solution.py:60
  33.9 5.6 %reshape.56 = bf16[4096,1,3,16]{3,2,1,0:T(4,128)(2,1)} reshape(bf16[32,2,3072]{2,1,0:T(2,128)(2,1)S(1)} %all-to-all-done) | data formatting | bytes 786432
  39.5 6.4 %copy.12 = bf16[1,16,3,32,128]{4,2,1,3,0:T(4,128)(2,1)S(1)} copy(bf16[1,16,3,32,128]{1,2,4,3,0:T(4,128)(2,1)} %bitcast.58) | data formatting | bytes 786432 | tf_op jit(solution)/shard_map/all_to_all | solution.py:60
  46.1 15.1 %while.11 = (s32[]{:T(128)}, bf16[2,256,128]{2,1,0:T(8,128)(2,1)S(1)}, bf16[2,256,128]{2,1,0:T(8,128)(2,1)S(1)}, bf16[512,128]{1,0:T(8,128)(2,1)S(1)}, bf16[8192...) while((s32[]{:T(128)}, ...), condition=%wide.region_5.6_spmd.clone, body=%wide.region_0.5_spmd.clone.sunk | while | flops 1156488704 | bytes 31686248 | solution.py:77
  46.1 0.8 compare_reduce_fusion.2
  46.8 3.0 %fusion.45 = (f32[256]{0:T(256)S(1)}, f32[256,8192]{1,0:T(8,128)S(1)}) fusion(bf16[8192,256]{1,0:T(8,128)(2,1)} %get-tuple-element.169, bf16[2,256,128]{2,1,0:T(8,128)(2,1)S(1)} %get-tuple-element.167, s32[]{:T(128)} %get-tuple-element.156, pred[8192]{0:T(1024)(128)(4,1)S(1)} %compare_reduce_fusion.2), kind=kOutput, calls=%fused_computation.34.clone.1 | convolution fusion | flops 543162112 | bytes 10561024 | tf_op jit(solution)/shard_map/while/body/eval_jaxpr/dot_general | solution.py:45
  50.2 1.4 %fusion.49 = f32[256]{0:T(256)S(1)} fusion(f32[256,8192]{1,0:T(8,128)S(1)} %get-tuple-element.143, f32[256]{0:T(256)S(1)} %max.10), kind=kLoop, calls=%fused_computation.4.clone.1 | loop fusion | flops 4194048 | bytes 8390656 | tf_op jit(solution)/shard_map/while/body/eval_jaxpr/reduce_sum | solution.py:23
  51.8 1.5 %fusion.47 = f32[256,128]{1,0:T(8,128)S(1)} fusion(bf16[8192,128]{1,0:T(8,128)(2,1)S(1)} %get-tuple-element.171, f32[256,8192]{1,0:T(8,128)S(1)} %get-tuple-element.143, f32[256]{0:T(256)S(1)} %max.10), kind=kOutput, calls=%fused_computation.6.clone.1 | convolution fusion | flops 541065216 | bytes 10617856 | tf_op jit(solution)/shard_map/while/body/eval_jaxpr/dot_general | solution.py:25
  53.6 0.8 compare_reduce_fusion.2
  54.4 3.0 %fusion.45 = (f32[256]{0:T(256)S(1)}, f32[256,8192]{1,0:T(8,128)S(1)}) fusion(bf16[8192,256]{1,0:T(8,128)(2,1)} %get-tuple-element.169, bf16[2,256,128]{2,1,0:T(8,128)(2,1)S(1)} %get-tuple-element.167, s32[]{:T(128)} %get-tuple-element.156, pred[8192]{0:T(1024)(128)(4,1)S(1)} %compare_reduce_fusion.2), kind=kOutput, calls=%fused_computation.34.clone.1 | convolution fusion | flops 543162112 | bytes 10561024 | tf_op jit(solution)/shard_map/while/body/eval_jaxpr/dot_general | solution.py:45
  57.4 0.3 fusion.46
  57.7 1.4 %fusion.49 = f32[256]{0:T(256)S(1)} fusion(f32[256,8192]{1,0:T(8,128)S(1)} %get-tuple-element.143, f32[256]{0:T(256)S(1)} %max.10), kind=kLoop, calls=%fused_computation.4.clone.1 | loop fusion | flops 4194048 | bytes 8390656 | tf_op jit(solution)/shard_map/while/body/eval_jaxpr/reduce_sum | solution.py:23
  59.3 1.5 %fusion.47 = f32[256,128]{1,0:T(8,128)S(1)} fusion(bf16[8192,128]{1,0:T(8,128)(2,1)S(1)} %get-tuple-element.171, f32[256,8192]{1,0:T(8,128)S(1)} %get-tuple-element.143, f32[256]{0:T(256)S(1)} %max.10), kind=kOutput, calls=%fused_computation.6.clone.1 | convolution fusion | flops 541065216 | bytes 10617856 | tf_op jit(solution)/shard_map/while/body/eval_jaxpr/dot_general | solution.py:25
  61.4 0.5 broadcast.62
  61.9 1.4 %reduce.2 = bf16[512,128]{1,0:T(8,128)(2,1)S(1)} reduce(bf16[512,1,128]{2,1,0:T(2,128)(2,1)S(1)} %bitcast.64, bf16[]{:T(256)} %broadcast.62), dimensions={1}, to_apply=%bitcast.43.reduce_sub_computation | reduce | bytes 262146
  63.3 11.2 %all_to_all.33 = bf16[32,2,1024]{2,1,0:T(2,128)(2,1)S(1)} all-to-all(bf16[32,2,1024]{2,1,0:T(2,128)(2,1)S(1)} %reshape.57), channel_id=1, replica_groups=mesh['section'=16,'seq'=32] {'seq'}, dimensions={0} | all-to-all | bytes 262144 | tf_op jit(solution)/shard_map/all_to_all | solution.py:80
  74.7 1.9 %collective-permute-start = (bf16[1,16,4096]{2,1,0:T(8,128)(2,1)S(1)}, bf16[1,16,4096]{2,1,0:T(8,128)(2,1)S(1)}, u32[]{:S(2)}, u32[]{:S(2)}) collective-permute-start(bf16[1,16,4096]{2,1,0:T(8,128)(2,1)S(1)} %bitcast.68), channel_id=1, source_target_pairs={{0,32},{32,64},{64,96},{96,128},{128,160},{160,192},{192,224},{224... | collective-permute-start | bytes 393224 | tf_op jit(solution)/shard_map/ppermute | solution.py:14
  76.6 10.8 %collective-permute-done = bf16[1,16,4096]{2,1,0:T(8,128)(2,1)S(1)} collective-permute-done((bf16[1,16,4096]{2,1,0:T(8,128)(2,1)S(1)}, bf16[1,16,4096]{2,1,0:T(8,128)(2,1)S(1)}, u32[]{:S(2)}, u32[]{:S(2)}) %collective-permute-start) | collective-permute-done | bytes 131104 | tf_op jit(solution)/shard_map/ppermute | solution.py:14
  87.4 0.7 copy.37
  (19 shorter events, 2.0 us)
Async XLA Ops:
  13.2 20.7 %all-to-all-start = ((bf16[32,2,3072]{2,1,0:T(2,128)(2,1)}), bf16[32,2,3072]{2,1,0:T(2,128)(2,1)S(1)}, u32[]{:S(2)}, u32[]{:S(2)}) async-start(bf16[32,2,3072]{2,1,0:T(2,128)(2,1)} %reshape.55), calls=%async_computation | async-start | bytes 786432 | tf_op jit(solution)/shard_map/all_to_all | solution.py:60
  26.3 1.9 %copy-start = (bf16[1024,8,2,128]{3,1,2,0:T(8,128)(2,1)}, bf16[1024,8,2,128]{3,1,2,0:T(8,128)(2,1)S(1)}, u32[]{:S(2)}) copy-start(bf16[1024,8,2,128]{3,1,2,0:T(8,128)(2,1)S(1)} %copy.23) | copy-start | bytes 12582916
  74.7 12.7 %collective-permute-start = (bf16[1,16,4096]{2,1,0:T(8,128)(2,1)S(1)}, bf16[1,16,4096]{2,1,0:T(8,128)(2,1)S(1)}, u32[]{:S(2)}, u32[]{:S(2)}) collective-permute-start(bf16[1,16,4096]{2,1,0:T(8,128)(2,1)S(1)} %bitcast.68), channel_id=1, source_target_pairs={{0,32},{32,64},{64,96},{96,128},{128,160},{160,192},{192,224},{224... | collective-permute-start | bytes 393224 | tf_op jit(solution)/shard_map/ppermute | solution.py:14
where the time goes:
time: 89 us; the launch traced here: 88.1 us
  local copies, waits for them, and re-layouts  31.7 us (36%)
  waiting for transfers between devices  16.3 us (18%)
  starting transfers between devices  12.3 us (14%)
  blocking collectives  11.2 us (13%)
  matrix products  10.3 us (12%)
  other arithmetic  6.13 us (7%)
    unnamed x12, local copies, waits for them, and re-layouts  24.9 us
    all_to_all x1, blocking collectives, body(): lax.all_to_all(attended, 'seq', split_axis=1, concat_axis=2, tiled=True)  11.2 us
    ppermute x1, waiting for transfers between devices, shifted(): return lax.ppermute(value, axis, pairs)  10.8 us
    all_to_all x1, starting transfers between devices, body(): lax.all_to_all(fresh, 'seq', split_axis=3, concat_axis=1, tiled=True)[0]  10.4 us
    all_to_all x1, local copies, waits for them, and re-layouts, body(): lax.all_to_all(fresh, 'seq', split_axis=3, concat_axis=1, tiled=True)[0]  6.38 us
    dot_general x2, matrix products, stale_scores(): lax.dot_general(qrows, keys, (((1,), (1,)), ((), ())), preferred_element_...  6.06 us
    all_to_all x1, waiting for transfers between devices, body(): lax.all_to_all(fresh, 'seq', split_axis=3, concat_axis=1, tiled=True)[0]  5.47 us
    dot_general x2, matrix products, combine(): jnp.dot(old_expo.astype(jnp.bfloat16), old_values, preferred_element_type...  3.02 us
  transfers between devices with their start and end apart: 2, of which 2 were waited for; matrix products, arithmetic and copies ran while one was open for 3% of the time, Pallas kernels for 0%

commit v1 on v0

v1 whole, which is shorter than its diff:
```python
import functools
import math

import jax
import jax.numpy as jnp
from jax import lax
from jax.experimental import pallas as pl
from jax.experimental.pallas import tpu as pltpu
from jax.sharding import PartitionSpec as P

HD = 128
FACTOR = HD**-0.5 * math.log2(math.e)


def attend_kernel(chunk, own_ref, qkv_ref, keys_ref, values_ref, out_ref):
    devices, rows, width = qkv_ref.shape
    tokens = rows // 3
    patch = devices * tokens
    count = keys_ref.shape[0] // chunk
    own = own_ref[0]

    def received(part):
        return qkv_ref[:, part * tokens : (part + 1) * tokens, :].reshape(patch, width)

    scaled = received(0).astype(jnp.float32) * FACTOR
    high = scaled.astype(jnp.bfloat16)
    low = (scaled - high.astype(jnp.float32)).astype(jnp.bfloat16)
    queries = jnp.concatenate([high, low], axis=1)
    new_keys = received(1)
    new_values = received(2)
    ones = jnp.ones((chunk, width), jnp.bfloat16)

    def block(ref, fresh, index):
        pieces = []
        for part in range(chunk // patch):
            slot = index * (chunk // patch) + part
            piece = ref[slot * patch : (slot + 1) * patch, :]
            pieces.append(jnp.where(own == slot, fresh, piece))
        return jnp.concatenate(pieces, axis=0)

    def score(index):
        keys = block(keys_ref, new_keys, index)
        keys = jnp.concatenate([keys, keys], axis=1)
        return lax.dot_general(
            queries, keys, (((1,), (1,)), ((), ())), preferred_element_type=jnp.float32
        )

    top = None
    summed = None
    scores = score(0)
    for index in range(count):
        later = score(index + 1) if index + 1 < count else None
        peak = jnp.max(scores, axis=1, keepdims=True)
        new_top = peak if top is None else jnp.maximum(top, peak)
        weights = jnp.exp2(scores - new_top).astype(jnp.bfloat16)
        values = jnp.concatenate([block(values_ref, new_values, index), ones], axis=1)
        term = jnp.dot(weights, values, preferred_element_type=jnp.float32)
        summed = term if top is None else summed * jnp.exp2(top - new_top) + term
        top = new_top
        scores = later
    out = summed[:, :width] / summed[:, width:]
    out_ref[...] = out.astype(jnp.bfloat16).reshape(out_ref.shape)


def attend(own, qkv, keys, values):
    devices, rows, width = qkv.shape
    tokens = rows // 3
    length = keys.shape[0]
    patch = devices * tokens
    vmem = pl.BlockSpec(memory_space=pltpu.VMEM)
    return pl.pallas_call(
        functools.partial(attend_kernel, 2 * patch),
        out_shape=jax.ShapeDtypeStruct((devices, tokens, width), jnp.bfloat16),
        in_specs=[pl.BlockSpec(memory_space=pltpu.SMEM), vmem, vmem, vmem],
        out_specs=vmem,
        compiler_params=pltpu.CompilerParams(vmem_limit_bytes=32 << 20),
        cost_estimate=pl.CostEstimate(
            flops=4 * patch * length * width,
            bytes_accessed=4 * length * width,
            transcendentals=patch * length,
        ),
        name="attend",
    )(own, qkv, keys, values)


def body(fresh, stale, section_patch):
    _, tokens, parts, total_width = fresh.shape
    _, slots, patch, _, width = stale.shape
    devices = lax.axis_size("seq")
    sections = lax.axis_size("section")

    packed = fresh[0].reshape(tokens, parts, devices, width)
    packed = packed.transpose(2, 1, 0, 3).reshape(devices, parts * tokens, width)
    qkv = lax.all_to_all(packed, "seq", split_axis=0, concat_axis=0, tiled=True)

    cache = stale[0].reshape(slots * patch, 2, width)
    attended = attend(section_patch, qkv, cache[:, 0], cache[:, 1])

    pairs = [(source, (source + 1) % sections) for source in range(sections)]
    handed = lax.ppermute(attended, "section", pairs)
    handed = lax.all_to_all(handed, "seq", split_axis=0, concat_axis=0, tiled=True)
    return handed.transpose(1, 0, 2).reshape(1, tokens, total_width)


def solution(mesh):
    return jax.shard_map(
        body,
        mesh=mesh,
        in_specs=(
            P("section", "seq", None, None),
            P("section", None, None, None, "seq"),
            P("section"),
        ),
        out_specs=P("section", "seq", None),
        check_vma=False,
    )
```

time: 89 us -> 55 us (0.62)
  local copies, waits for them, and re-layouts: 31.7 us -> 9.05 us
  matrix products: 10.3 us -> 0 us
  other arithmetic: 6.13 us -> 0 us
  Pallas kernels: 0 us -> 5.38 us
    unnamed x12 -> x4, local copies, waits for them, and re-layouts: 24.9 us -> 5.81 us
    dot_general x8 -> x0, matrix products: 10.3 us -> none  [the longest x2 6.06 us: stale_scores(): lax.dot_general(qrows, keys, (((1,), (1,)), ((), ())), preferred_element_...]
    all_to_all x2 -> x0, local copies, waits for them, and re-layouts: 6.39 us -> none  [the longest x1 6.38 us: body(): lax.all_to_all(fresh, 'seq', split_axis=3, concat_axis=1, tiled=True)[0]]
    pallas_call x0 -> x1, Pallas kernels: none -> 5.38 us  [attend(): pl.pallas_call(functools.partial(attend_kernel, 2 * patch), out_shape=jax...]
    reduce_sum x4 -> x0, other arithmetic: 3.16 us -> none  [the longest x2 2.71 us: combine(): jnp.sum(old_expo, axis=-1, keepdims=True)]
    squeeze x0 -> x1, local copies, waits for them, and re-layouts: none -> 1.6 us  [body(): attended = attend(section_patch, qkv, cache[:, 0], cache[:, 1])]
    eq x2 -> x0, other arithmetic: 1.53 us -> none  [body(): hidden_slot = (slot_ids == own)[None, :]]
    unnamed x1 -> x0, other arithmetic: 1.41 us -> none
  transfers between devices with their start and end apart: 2 -> 2, of which waited for: 2 -> 2; matrix products, arithmetic and copies ran while one was open for 3% -> 9% of each run, Pallas kernels for 0% -> 0%
where the time goes in v1:
time: 55 us; the launch traced here: 54.7 us
  waiting for transfers between devices  15.7 us (29%)
  starting transfers between devices  12.3 us (22%)
  blocking collectives  11.5 us (21%)
  local copies, waits for them, and re-layouts  9.05 us (16%)
  Pallas kernels  5.38 us (10%)
  between operations  0.7 us (1%)
    all_to_all x1, blocking collectives, body(): lax.all_to_all(handed, 'seq', split_axis=0, concat_axis=0, tiled=True)  11.5 us
    ppermute x1, waiting for transfers between devices, body(): handed = lax.ppermute(attended, 'section', pairs)  10.8 us
    all_to_all x1, starting transfers between devices, body(): qkv = lax.all_to_all(packed, 'seq', split_axis=0, concat_axis=0, tiled=True)  10.4 us
    unnamed x4, local copies, waits for them, and re-layouts  5.81 us
    pallas_call x1, Pallas kernels, attend(): pl.pallas_call(functools.partial(attend_kernel, 2 * patch), out_shape=jax...  5.38 us
    all_to_all x1, waiting for transfers between devices, body(): qkv = lax.all_to_all(packed, 'seq', split_axis=0, concat_axis=0, tiled=True)  4.86 us
    ppermute x1, starting transfers between devices, body(): handed = lax.ppermute(attended, 'section', pairs)  1.92 us
    squeeze x1, local copies, waits for them, and re-layouts, body(): attended = attend(section_patch, qkv, cache[:, 0], cache[:, 1])  1.6 us
  transfers between devices with their start and end apart: 2, of which 2 were waited for; matrix products, arithmetic and copies ran while one was open for 9% of the time, Pallas kernels for 0%

profile of v1, /device:TPU:1, one launch (start us, length us, event | category | flops | bytes accessed | tf_op | source)
XLA Modules:
  0.0 54.7 jit_solution(4721256312292308159)
XLA Ops:
  0.0 1.1 %copy.9 = bf16[6,8,32,128]{3,2,1,0:T(8,128)(2,1)S(1)} copy(bf16[6,8,32,128]{3,1,2,0:T(8,128)(2,1)} %bitcast.19) | data formatting | bytes 786432
  1.1 0.9 %copy.6 = bf16[16,3,32,128]{3,0,1,2:T(8,128)(2,1)} copy(bf16[16,3,32,128]{3,2,0,1:T(8,128)(2,1)S(1)} %bitcast.17) | data formatting | bytes 786432 | tf_op jit(solution)/shard_map/reshape;squeeze | solution.py:92
  2.0 10.4 %all-to-all-start = ((bf16[32,48,128]{2,1,0:T(8,128)(2,1)}), bf16[32,48,128]{2,1,0:T(8,128)(2,1)S(1)}, u32[]{:S(2)}, u32[]{:S(2)}) async-start(bf16[32,48,128]{2,1,0:T(8,128)(2,1)} %bitcast.1), calls=%async_computation | async-start | bytes 786432 | tf_op jit(solution)/shard_map/all_to_all | solution.py:94
  12.4 3.2 %copy.7 = bf16[1,16,512,2,128]{4,2,1,3,0:T(8,128)(2,1)S(1)} copy(bf16[1,16,512,2,128]{4,3,2,1,0:T(2,128)(2,1)} %param.4) | data formatting | bytes 8388608 | tf_op args[1]
  15.5 1.6 %slice_bitcast_fusion = (bf16[8192,128]{1,0:T(8,128)(2,1)S(1)}, bf16[8192,128]{1,0:T(8,128)(2,1)}) fusion(bf16[8192,2,128]{2,0,1:T(8,128)(2,1)S(1)} %bitcast.16), kind=kLoop, calls=%fused_computation | loop fusion | bytes 8388608 | tf_op jit(solution)/shard_map/squeeze | solution.py:97
  17.8 4.9 %all-to-all-done.qkv_ref = bf16[32,48,128]{2,1,0:T(8,128)(2,1)S(1)} async-done(((bf16[32,48,128]{2,1,0:T(8,128)(2,1)}), bf16[32,48,128]{2,1,0:T(8,128)(2,1)S(1)}, u32[]{:S(2)}, u32[]{:S(2)}) %all-to-all-start) | async-done | bytes 393248 | tf_op jit(solution)/shard_map/all_to_all | solution.py:94
  22.7 0.0 copy-start
  22.7 1.6 %copy-done = bf16[8192,128]{1,0:T(8,128)(2,1)S(1)} copy-done((bf16[8192,128]{1,0:T(8,128)(2,1)S(1)}, bf16[8192,128]{1,0:T(8,128)(2,1)}, u32[]{:S(2)}) %copy-start) | copy-done | bytes 2097176
  24.2 5.4 %attend.1 = bf16[32,16,128]{2,1,0:T(8,128)(2,1)S(1)} custom-call(s32[1]{0:T(128)S(6)} %copy.10.own_ref, bf16[32,48,128]{2,1,0:T(8,128)(2,1)S(1)} %all-to-all-done.qkv_ref, bf16[8192,128]{1,0:T(8,128)(2,1)S(1)} %copy-done, bf16[8192,128]{1,0:T(8,128)(2,1)S(1)} %get-tuple-element.5.values_ref), custom_call_target="tpu_custom_call" | custom-call | flops 2147483648 | bytes 4194304 | tf_op jit(solution)/shard_map/attend/pallas_call | solution.py:71
  29.6 1.9 %collective-permute-start = (bf16[32,16,128]{2,1,0:T(8,128)(2,1)S(1)}, bf16[32,16,128]{2,1,0:T(8,128)(2,1)S(1)}, u32[]{:S(2)}, u32[]{:S(2)}) collective-permute-start(bf16[32,16,128]{2,1,0:T(8,128)(2,1)S(1)} %attend.1), channel_id=1, source_target_pairs={{0,32},{32,64},{64,96},{96,128},{128,160},{160,192},{192,224},{224... | collective-permute-start | bytes 393224 | tf_op jit(solution)/shard_map/ppermute | solution.py:100
  31.6 10.8 %collective-permute-done = bf16[32,16,128]{2,1,0:T(8,128)(2,1)S(1)} collective-permute-done((bf16[32,16,128]{2,1,0:T(8,128)(2,1)S(1)}, bf16[32,16,128]{2,1,0:T(8,128)(2,1)S(1)}, u32[]{:S(2)}, u32[]{:S(2)}) %collective-permute-start) | collective-permute-done | bytes 131104 | tf_op jit(solution)/shard_map/ppermute | solution.py:100
  42.4 11.5 %all_to_all.10 = bf16[32,16,128]{2,1,0:T(8,128)(2,1)S(1)} all-to-all(bf16[32,16,128]{2,1,0:T(8,128)(2,1)S(1)} %collective-permute-done), channel_id=1, replica_groups=mesh['section'=16,'seq'=32] {'seq'}, dimensions={0} | all-to-all | bytes 262144 | tf_op jit(solution)/shard_map/all_to_all | solution.py:101
  54.0 0.7 %reshape.7 = bf16[1,16,4096]{2,1,0:T(8,128)(2,1)} reshape(bf16[16,32,128]{2,1,0:T(8,128)(2,1)S(1)} %copy.8) | data formatting | bytes 262144 | tf_op jit(solution)/shard_map/reshape | solution.py:102
  (1 shorter events, 0.0 us)
Async XLA Ops:
  2.0 20.7 %all-to-all-start = ((bf16[32,48,128]{2,1,0:T(8,128)(2,1)}), bf16[32,48,128]{2,1,0:T(8,128)(2,1)S(1)}, u32[]{:S(2)}, u32[]{:S(2)}) async-start(bf16[32,48,128]{2,1,0:T(8,128)(2,1)} %bitcast.1), calls=%async_computation | async-start | bytes 786432 | tf_op jit(solution)/shard_map/all_to_all | solution.py:94
  22.7 1.6 %copy-start = (bf16[8192,128]{1,0:T(8,128)(2,1)S(1)}, bf16[8192,128]{1,0:T(8,128)(2,1)}, u32[]{:S(2)}) copy-start(bf16[8192,128]{1,0:T(8,128)(2,1)} %get-tuple-element.6.keys_ref) | copy-start | bytes 6291460
  29.6 12.8 %collective-permute-start = (bf16[32,16,128]{2,1,0:T(8,128)(2,1)S(1)}, bf16[32,16,128]{2,1,0:T(8,128)(2,1)S(1)}, u32[]{:S(2)}, u32[]{:S(2)}) collective-permute-start(bf16[32,16,128]{2,1,0:T(8,128)(2,1)S(1)} %attend.1), channel_id=1, source_target_pairs={{0,32},{32,64},{64,96},{96,128},{128,160},{160,192},{192,224},{224... | collective-permute-start | bytes 393224 | tf_op jit(solution)/shard_map/ppermute | solution.py:100

commit v2 on v1

v2 whole, which is shorter than its diff:
```python
import functools
import math

import jax
import jax.numpy as jnp
from jax import lax
from jax.experimental import pallas as pl
from jax.experimental.pallas import tpu as pltpu
from jax.sharding import PartitionSpec as P

HD = 128
CHUNK = 1024
FACTOR = HD**-0.5 * math.log2(math.e)


def attend_kernel(
    chunk, own_ref, qkv_ref, keys_ref, front_ref, back_hbm, out_ref, back_ref,
    weights_ref, decay_ref, summed_ref, sem
):
    devices, rows, width = qkv_ref.shape
    tokens = rows // 3
    patch = devices * tokens
    count = keys_ref.shape[0] // chunk
    half = front_ref.shape[0]
    own = own_ref[0]
    fetch = pltpu.make_async_copy(back_hbm, back_ref, sem)
    fetch.start()

    def received(part):
        return qkv_ref[:, part * tokens : (part + 1) * tokens, :].reshape(patch, width)

    scaled = received(0).astype(jnp.float32) * FACTOR
    high = scaled.astype(jnp.bfloat16)
    low = (scaled - high.astype(jnp.float32)).astype(jnp.bfloat16)
    queries = jnp.concatenate([high, low], axis=1)
    new_keys = received(1)
    new_values = received(2)
    ones = jnp.ones((chunk, width), jnp.bfloat16)

    def block(ref, first, fresh, index):
        pieces = []
        for start in range(index * chunk, (index + 1) * chunk, patch):
            piece = ref[start - first : start - first + patch, :]
            pieces.append(jnp.where(own == start // patch, fresh, piece))
        return jnp.concatenate(pieces, axis=0)

    def score(index):
        keys = block(keys_ref, 0, new_keys, index)
        keys = jnp.concatenate([keys, keys], axis=1)
        return lax.dot_general(
            queries, keys, (((1,), (1,)), ((), ())), preferred_element_type=jnp.float32
        )

    def accumulate(summed, weights, decay, values):
        values = jnp.concatenate([values, ones], axis=1)
        term = jnp.dot(weights, values, preferred_element_type=jnp.float32)
        return term if summed is None else summed * decay + term

    @pl.when(own >= 0)
    def first():
        top = None
        decay = None
        summed = None
        scores = score(0)
        for index in range(count):
            later = score(index + 1) if index + 1 < count else None
            peak = jnp.max(scores, axis=1, keepdims=True)
            new_top = peak if top is None else jnp.maximum(top, peak)
            weights = jnp.exp2(scores - new_top).astype(jnp.bfloat16)
            if top is not None:
                decay = jnp.exp2(top - new_top)
            if index * chunk < half:
                values = block(front_ref, 0, new_values, index)
                summed = accumulate(summed, weights, decay, values)
            else:
                weights_ref[index - half // chunk] = weights
                decay_ref[index - half // chunk] = jnp.broadcast_to(decay, (patch, width))
            top = new_top
            scores = later
        summed_ref[...] = summed

    fetch.wait()
    summed = summed_ref[...]
    for index in range(half // chunk, count):
        values = block(back_ref, half, new_values, index)
        decay = decay_ref[index - half // chunk]
        decay = jnp.concatenate([decay, decay], axis=1)
        summed = accumulate(summed, weights_ref[index - half // chunk], decay, values)
    out = summed[:, :width] / summed[:, width:]
    out_ref[...] = out.astype(jnp.bfloat16).reshape(out_ref.shape)


def attend(own, qkv, keys, front, back):
    devices, rows, width = qkv.shape
    tokens = rows // 3
    length = keys.shape[0]
    patch = devices * tokens
    vmem = pl.BlockSpec(memory_space=pltpu.VMEM)
    return pl.pallas_call(
        functools.partial(attend_kernel, CHUNK),
        out_shape=jax.ShapeDtypeStruct((devices, tokens, width), jnp.bfloat16),
        in_specs=[
            pl.BlockSpec(memory_space=pltpu.SMEM),
            vmem,
            vmem,
            vmem,
            pl.BlockSpec(memory_space=pltpu.HBM),
        ],
        out_specs=vmem,
        scratch_shapes=[
            pltpu.VMEM(back.shape, back.dtype),
            pltpu.VMEM((length // CHUNK // 2, patch, CHUNK), jnp.bfloat16),
            pltpu.VMEM((length // CHUNK // 2, patch, width), jnp.float32),
            pltpu.VMEM((patch, 2 * width), jnp.float32),
            pltpu.SemaphoreType.DMA,
        ],
        compiler_params=pltpu.CompilerParams(vmem_limit_bytes=36 << 20),
        cost_estimate=pl.CostEstimate(
            flops=4 * patch * length * width,
            bytes_accessed=4 * length * width,
            transcendentals=patch * length,
        ),
        name="attend",
    )(own, qkv, keys, front, back)


def body(fresh, stale, section_patch):
    _, tokens, parts, total_width = fresh.shape
    _, slots, patch, _, width = stale.shape
    devices = lax.axis_size("seq")
    sections = lax.axis_size("section")

    packed = fresh[0].reshape(tokens // 8, 8, parts, devices, width)
    packed = packed.transpose(3, 2, 0, 1, 4).reshape(devices, parts * tokens, width)
    qkv = lax.all_to_all(packed, "seq", split_axis=0, concat_axis=0, tiled=True)

    cache = stale[0].reshape(slots * patch, 2, width)
    half = slots // 2 * patch
    keys, front, back = cache[:, 0], cache[:half, 1], cache[half:, 1]
    back = pltpu.with_memory_space_constraint(back, pltpu.HBM)
    attended = attend(section_patch, qkv, keys, front, back)

    pairs = [(source, (source + 1) % sections) for source in range(sections)]
    handed = lax.ppermute(attended, "section", pairs)
    handed = lax.all_to_all(handed, "seq", split_axis=0, concat_axis=0, tiled=True)
    handed = handed.reshape(devices, tokens // 8, 8, width).transpose(1, 2, 0, 3)
    return handed.reshape(1, tokens, total_width)


def solution(mesh):
    return jax.shard_map(
        body,
        mesh=mesh,
        in_specs=(
            P("section", "seq", None, None),
            P("section", None, None, None, "seq"),
            P("section"),
        ),
        out_specs=P("section", "seq", None),
        check_vma=False,
    )
```

time: 55 us -> 53.7 us (0.976)
  local copies, waits for them, and re-layouts: 9.05 us -> 6.89 us
  Pallas kernels: 5.38 us -> 5.94 us
    unnamed x4 -> x1, local copies, waits for them, and re-layouts: 5.81 us -> 3.16 us
    another operation x1, local copies, waits for them, and re-layouts: 0.89 us -> 1.82 us  [body(): packed = fresh[0].reshape(tokens // 8, 8, parts, devices, width)]
    pallas_call x1, Pallas kernels: 5.38 us -> 5.94 us  [attend(): pl.pallas_call(functools.partial(attend_kernel, CHUNK), out_shape=jax.Sha...]
    squeeze x1 -> x2, local copies, waits for them, and re-layouts: 1.6 us -> 1.24 us  [body(): keys, front, back = (cache[:, 0], cache[:half, 1], cache[half:, 1])]
  transfers between devices with their start and end apart: 2 -> 2, of which waited for: 2 -> 2; matrix products, arithmetic and copies ran while one was open for 9% -> 8% of each run, Pallas kernels for 0% -> 0%
where the time goes in v2:
time: 53.7 us; the launch traced here: 53.4 us
  waiting for transfers between devices  16 us (30%)
  starting transfers between devices  12.3 us (23%)
  blocking collectives  11.5 us (21%)
  local copies, waits for them, and re-layouts  6.89 us (13%)
  Pallas kernels  5.94 us (11%)
  between operations  0.69 us (1%)
    all_to_all x1, blocking collectives, body(): lax.all_to_all(handed, 'seq', split_axis=0, concat_axis=0, tiled=True)  11.5 us
    ppermute x1, waiting for transfers between devices, body(): handed = lax.ppermute(attended, 'section', pairs)  10.8 us
    all_to_all x1, starting transfers between devices, body(): qkv = lax.all_to_all(packed, 'seq', split_axis=0, concat_axis=0, tiled=True)  10.4 us
    pallas_call x1, Pallas kernels, attend(): pl.pallas_call(functools.partial(attend_kernel, CHUNK), out_shape=jax.Sha...  5.94 us
    all_to_all x1, waiting for transfers between devices, body(): qkv = lax.all_to_all(packed, 'seq', split_axis=0, concat_axis=0, tiled=True)  5.21 us
    unnamed x1, local copies, waits for them, and re-layouts  3.16 us
    ppermute x1, starting transfers between devices, body(): handed = lax.ppermute(attended, 'section', pairs)  1.92 us
    another operation x1, local copies, waits for them, and re-layouts, body(): packed = fresh[0].reshape(tokens // 8, 8, parts, devices, width)  1.82 us
  transfers between devices with their start and end apart: 2, of which 2 were waited for; matrix products, arithmetic and copies ran while one was open for 8% of the time, Pallas kernels for 0%

profile of v2, /device:TPU:1, one launch (start us, length us, event | category | flops | bytes accessed | tf_op | source)
XLA Modules:
  0.0 53.4 jit_solution(10327453056012731734)
XLA Ops:
  0.0 1.8 %copy.4 = bf16[2,8,3,32,128]{4,1,0,2,3:T(8,128)(2,1)} copy(bf16[2,8,3,32,128]{4,1,3,0,2:T(8,128)(2,1)} %bitcast.20) | data formatting | bytes 786432 | tf_op jit(solution)/shard_map/reshape;squeeze | solution.py:133
  1.8 10.4 %all-to-all-start = ((bf16[32,48,128]{2,1,0:T(8,128)(2,1)}), bf16[32,48,128]{2,1,0:T(8,128)(2,1)S(1)}, u32[]{:S(2)}, u32[]{:S(2)}) async-start(bf16[32,48,128]{2,1,0:T(8,128)(2,1)} %bitcast.2), calls=%async_computation | async-start | bytes 786432 | tf_op jit(solution)/shard_map/all_to_all | solution.py:135
  12.2 3.2 %copy.5 = bf16[1,16,512,2,128]{4,2,1,3,0:T(8,128)(2,1)S(1)} copy(bf16[1,16,512,2,128]{4,3,2,1,0:T(2,128)(2,1)} %param.4) | data formatting | bytes 8388608 | tf_op args[1]
  15.4 0.1 slice_bitcast_fusion.keys_ref
  15.6 1.1 %slice_bitcast_fusion.1 = (bf16[4096,128]{1,0:T(8,128)(2,1)}, bf16[4096,128]{1,0:T(8,128)(2,1)S(1)}) fusion(bf16[8192,2,128]{2,0,1:T(8,128)(2,1)S(1)} %bitcast.19), kind=kLoop, calls=%fused_computation.1 | loop fusion | bytes 4194304 | tf_op jit(solution)/shard_map/squeeze | solution.py:139
  17.3 5.2 %all-to-all-done.qkv_ref = bf16[32,48,128]{2,1,0:T(8,128)(2,1)S(1)} async-done(((bf16[32,48,128]{2,1,0:T(8,128)(2,1)}), bf16[32,48,128]{2,1,0:T(8,128)(2,1)S(1)}, u32[]{:S(2)}, u32[]{:S(2)}) %all-to-all-start) | async-done | bytes 393248 | tf_op jit(solution)/shard_map/all_to_all | solution.py:135
  22.5 5.9 %attend.1 = bf16[32,16,128]{2,1,0:T(8,128)(2,1)S(1)} custom-call(s32[1]{0:T(128)S(6)} %copy.8.own_ref, bf16[32,48,128]{2,1,0:T(8,128)(2,1)S(1)} %all-to-all-done.qkv_ref, bf16[8192,128]{1,0:T(8,128)(2,1)S(1)} %slice_bitcast_fusion.keys_ref, bf16[4096,128]{1,0:T(8,128)(2,1)S(1)} %get-tuple-element.6.front_ref, bf16[4096,128]{1,0:T(8,128)(2,1)} %get-tuple-element.5.back_hbm), custom_call_target="tpu_custom_call" | custom-call | flops 2147483648 | bytes 4194304 | tf_op jit(solution)/shard_map/attend/pallas_call | solution.py:99
  28.5 1.9 %collective-permute-start = (bf16[32,16,128]{2,1,0:T(8,128)(2,1)S(1)}, bf16[32,16,128]{2,1,0:T(8,128)(2,1)S(1)}, u32[]{:S(2)}, u32[]{:S(2)}) collective-permute-start(bf16[32,16,128]{2,1,0:T(8,128)(2,1)S(1)} %attend.1), channel_id=1, source_target_pairs={{0,32},{32,64},{64,96},{96,128},{128,160},{160,192},{192,224},{224... | collective-permute-start | bytes 393224 | tf_op jit(solution)/shard_map/ppermute | solution.py:144
  30.4 10.8 %collective-permute-done = bf16[32,16,128]{2,1,0:T(8,128)(2,1)S(1)} collective-permute-done((bf16[32,16,128]{2,1,0:T(8,128)(2,1)S(1)}, bf16[32,16,128]{2,1,0:T(8,128)(2,1)S(1)}, u32[]{:S(2)}, u32[]{:S(2)}) %collective-permute-start) | collective-permute-done | bytes 131104 | tf_op jit(solution)/shard_map/ppermute | solution.py:144
  41.2 11.5 %all_to_all.10 = bf16[32,16,128]{2,1,0:T(8,128)(2,1)S(1)} all-to-all(bf16[32,16,128]{2,1,0:T(8,128)(2,1)S(1)} %collective-permute-done), channel_id=1, replica_groups=mesh['section'=16,'seq'=32] {'seq'}, dimensions={0} | all-to-all | bytes 262144 | tf_op jit(solution)/shard_map/all_to_all | solution.py:145
  52.7 0.7 %copy_bitcast_fusion = bf16[1,16,4096]{2,1,0:T(8,128)(2,1)} fusion(bf16[32,16,128]{2,1,0:T(8,128)(2,1)S(1)} %all_to_all.10), kind=kLoop, calls=%fused_computation.3 | loop fusion | bytes 262144 | tf_op jit(solution)/shard_map/reshape | solution.py:147
Async XLA Ops:
  1.8 20.7 %all-to-all-start = ((bf16[32,48,128]{2,1,0:T(8,128)(2,1)}), bf16[32,48,128]{2,1,0:T(8,128)(2,1)S(1)}, u32[]{:S(2)}, u32[]{:S(2)}) async-start(bf16[32,48,128]{2,1,0:T(8,128)(2,1)} %bitcast.2), calls=%async_computation | async-start | bytes 786432 | tf_op jit(solution)/shard_map/all_to_all | solution.py:135
  28.5 12.8 %collective-permute-start = (bf16[32,16,128]{2,1,0:T(8,128)(2,1)S(1)}, bf16[32,16,128]{2,1,0:T(8,128)(2,1)S(1)}, u32[]{:S(2)}, u32[]{:S(2)}) collective-permute-start(bf16[32,16,128]{2,1,0:T(8,128)(2,1)S(1)} %attend.1), channel_id=1, source_target_pairs={{0,32},{32,64},{64,96},{96,128},{128,160},{160,192},{192,224},{224... | collective-permute-start | bytes 393224 | tf_op jit(solution)/shard_map/ppermute | solution.py:144

commit v3 on v2

--- a/solution.py
+++ b/solution.py
@@ -9,13 +9,13 @@
 from jax.sharding import PartitionSpec as P
 
 HD = 128
-CHUNK = 1024
+CHUNK = 2048
 FACTOR = HD**-0.5 * math.log2(math.e)
 
 
 def attend_kernel(
     chunk, own_ref, qkv_ref, keys_ref, front_ref, back_hbm, out_ref, back_ref,
-    weights_ref, decay_ref, summed_ref, sem
+    scores_ref, top_ref, sem
 ):
     devices, rows, width = qkv_ref.shape
     tokens = rows // 3
@@ -29,10 +29,7 @@
     def received(part):
         return qkv_ref[:, part * tokens : (part + 1) * tokens, :].reshape(patch, width)
 
-    scaled = received(0).astype(jnp.float32) * FACTOR
-    high = scaled.astype(jnp.bfloat16)
-    low = (scaled - high.astype(jnp.float32)).astype(jnp.bfloat16)
-    queries = jnp.concatenate([high, low], axis=1)
+    queries = received(0)
     new_keys = received(1)
     new_values = received(2)
     ones = jnp.ones((chunk, width), jnp.bfloat16)
@@ -41,12 +38,13 @@
         pieces = []
         for start in range(index * chunk, (index + 1) * chunk, patch):
             piece = ref[start - first : start - first + patch, :]
-            pieces.append(jnp.where(own == start // patch, fresh, piece))
+            if ref is not back_ref:
+                piece = jnp.where(own == start // patch, fresh, piece)
+            pieces.append(piece)
         return jnp.concatenate(pieces, axis=0)
 
     def score(index):
         keys = block(keys_ref, 0, new_keys, index)
-        keys = jnp.concatenate([keys, keys], axis=1)
         return lax.dot_general(
             queries, keys, (((1,), (1,)), ((), ())), preferred_element_type=jnp.float32
         )
@@ -54,38 +52,49 @@
     def accumulate(summed, weights, decay, values):
         values = jnp.concatenate([values, ones], axis=1)
         term = jnp.dot(weights, values, preferred_element_type=jnp.float32)
-        return term if summed is None else summed * decay + term
+        if summed is None:
+            return term
+        return (summed if decay is None else summed * decay) + term
+
+    held = half // chunk
 
     @pl.when(own >= 0)
     def first():
         top = None
-        decay = None
-        summed = None
-        scores = score(0)
-        for index in range(count):
-            later = score(index + 1) if index + 1 < count else None
+        for index in range(held):
+            scores = score(index)
+            scores_ref[index] = scores
             peak = jnp.max(scores, axis=1, keepdims=True)
-            new_top = peak if top is None else jnp.maximum(top, peak)
-            weights = jnp.exp2(scores - new_top).astype(jnp.bfloat16)
-            if top is not None:
-                decay = jnp.exp2(top - new_top)
-            if index * chunk < half:
-                values = block(front_ref, 0, new_values, index)
-                summed = accumulate(summed, weights, decay, values)
-            else:
-                weights_ref[index - half // chunk] = weights
-                decay_ref[index - half // chunk] = jnp.broadcast_to(decay, (patch, width))
-            top = new_top
-            scores = later
-        summed_ref[...] = summed
+            top = peak if top is None else jnp.maximum(top, peak)
+        top_ref[...] = jnp.broadcast_to(top, (patch, width))
 
     fetch.wait()
-    summed = summed_ref[...]
-    for index in range(half // chunk, count):
-        values = block(back_ref, half, new_values, index)
-        decay = decay_ref[index - half // chunk]
-        decay = jnp.concatenate([decay, decay], axis=1)
-        summed = accumulate(summed, weights_ref[index - half // chunk], decay, values)
+
+    @pl.when(own >= half // patch)
+    def replace():
+        start = pl.multiple_of(own * patch - half, patch)
+        back_ref[pl.ds(start, patch), :] = new_values
+
+    top = top_ref[:, :1]
+    decay = None
+    summed = None
+    later = []
+    for index in range(count):
+        if index < held:
+            later.append(score(held + index))
+            scores = scores_ref[index]
+        else:
+            scores = later[index - held]
+            peak = jnp.max(scores, axis=1, keepdims=True)
+            new_top = jnp.maximum(top, peak)
+            decay = jnp.exp2((top - new_top) * FACTOR)
+            top = new_top
+        weights = jnp.exp2((scores - top) * FACTOR).astype(jnp.bfloat16)
+        if index < held:
+            values = block(front_ref, 0, new_values, index)
+        else:
+            values = block(back_ref, half, new_values, index)
+        summed = accumulate(summed, weights, decay, values)
     out = summed[:, :width] / summed[:, width:]
     out_ref[...] = out.astype(jnp.bfloat16).reshape(out_ref.shape)
 
@@ -109,9 +118,8 @@
         out_specs=vmem,
         scratch_shapes=[
             pltpu.VMEM(back.shape, back.dtype),
-            pltpu.VMEM((length // CHUNK // 2, patch, CHUNK), jnp.bfloat16),
-            pltpu.VMEM((length // CHUNK // 2, patch, width), jnp.float32),
-            pltpu.VMEM((patch, 2 * width), jnp.float32),
+            pltpu.VMEM((length // CHUNK // 2, patch, CHUNK), jnp.float32),
+            pltpu.VMEM((patch, width), jnp.float32),
             pltpu.SemaphoreType.DMA,
         ],
         compiler_params=pltpu.CompilerParams(vmem_limit_bytes=36 << 20),

time: 53.7 us -> 52.9 us (0.985)
  Pallas kernels: 5.94 us -> 5.07 us
    pallas_call x1, Pallas kernels: 5.94 us -> 5.07 us  [attend(): pl.pallas_call(functools.partial(attend_kernel, CHUNK), out_shape=jax.Sha...]
where the time goes in v3:
time: 52.9 us; the launch traced here: 52.5 us
  waiting for transfers between devices  16 us (30%)
  starting transfers between devices  12.3 us (23%)
  blocking collectives  11.5 us (22%)
  local copies, waits for them, and re-layouts  6.89 us (13%)
  Pallas kernels  5.07 us (10%)
  between operations  0.69 us (1%)
    all_to_all x1, blocking collectives, body(): lax.all_to_all(handed, 'seq', split_axis=0, concat_axis=0, tiled=True)  11.5 us
    ppermute x1, waiting for transfers between devices, body(): handed = lax.ppermute(attended, 'section', pairs)  10.8 us
    all_to_all x1, starting transfers between devices, body(): qkv = lax.all_to_all(packed, 'seq', split_axis=0, concat_axis=0, tiled=True)  10.4 us
    all_to_all x1, waiting for transfers between devices, body(): qkv = lax.all_to_all(packed, 'seq', split_axis=0, concat_axis=0, tiled=True)  5.21 us
    pallas_call x1, Pallas kernels, attend(): pl.pallas_call(functools.partial(attend_kernel, CHUNK), out_shape=jax.Sha...  5.07 us
    unnamed x1, local copies, waits for them, and re-layouts  3.16 us
    ppermute x1, starting transfers between devices, body(): handed = lax.ppermute(attended, 'section', pairs)  1.92 us
    another operation x1, local copies, waits for them, and re-layouts, body(): packed = fresh[0].reshape(tokens // 8, 8, parts, devices, width)  1.82 us
  transfers between devices with their start and end apart: 2, of which 2 were waited for; matrix products, arithmetic and copies ran while one was open for 8% of the time, Pallas kernels for 0%

profile of v3, /device:TPU:1, one launch (start us, length us, event | category | flops | bytes accessed | tf_op | source)
XLA Modules:
  0.0 52.5 jit_solution(1298902571473883407)
XLA Ops:
  0.0 1.8 %copy.4 = bf16[2,8,3,32,128]{4,1,0,2,3:T(8,128)(2,1)} copy(bf16[2,8,3,32,128]{4,1,3,0,2:T(8,128)(2,1)} %bitcast.20) | data formatting | bytes 786432 | tf_op jit(solution)/shard_map/reshape;squeeze | solution.py:141
  1.8 10.4 %all-to-all-start = ((bf16[32,48,128]{2,1,0:T(8,128)(2,1)}), bf16[32,48,128]{2,1,0:T(8,128)(2,1)S(1)}, u32[]{:S(2)}, u32[]{:S(2)}) async-start(bf16[32,48,128]{2,1,0:T(8,128)(2,1)} %bitcast.2), calls=%async_computation | async-start | bytes 786432 | tf_op jit(solution)/shard_map/all_to_all | solution.py:143
  12.2 3.2 %copy.5 = bf16[1,16,512,2,128]{4,2,1,3,0:T(8,128)(2,1)S(1)} copy(bf16[1,16,512,2,128]{4,3,2,1,0:T(2,128)(2,1)} %param.4) | data formatting | bytes 8388608 | tf_op args[1]
  15.4 0.1 slice_bitcast_fusion.keys_ref
  15.6 1.1 %slice_bitcast_fusion.1 = (bf16[4096,128]{1,0:T(8,128)(2,1)}, bf16[4096,128]{1,0:T(8,128)(2,1)S(1)}) fusion(bf16[8192,2,128]{2,0,1:T(8,128)(2,1)S(1)} %bitcast.19), kind=kLoop, calls=%fused_computation.1 | loop fusion | bytes 4194304 | tf_op jit(solution)/shard_map/squeeze | solution.py:147
  17.3 5.2 %all-to-all-done.qkv_ref = bf16[32,48,128]{2,1,0:T(8,128)(2,1)S(1)} async-done(((bf16[32,48,128]{2,1,0:T(8,128)(2,1)}), bf16[32,48,128]{2,1,0:T(8,128)(2,1)S(1)}, u32[]{:S(2)}, u32[]{:S(2)}) %all-to-all-start) | async-done | bytes 393248 | tf_op jit(solution)/shard_map/all_to_all | solution.py:143
  22.5 5.1 %attend.1 = bf16[32,16,128]{2,1,0:T(8,128)(2,1)S(1)} custom-call(s32[1]{0:T(128)S(6)} %copy.8.own_ref, bf16[32,48,128]{2,1,0:T(8,128)(2,1)S(1)} %all-to-all-done.qkv_ref, bf16[8192,128]{1,0:T(8,128)(2,1)S(1)} %slice_bitcast_fusion.keys_ref, bf16[4096,128]{1,0:T(8,128)(2,1)S(1)} %get-tuple-element.6.front_ref, bf16[4096,128]{1,0:T(8,128)(2,1)} %get-tuple-element.5.back_hbm), custom_call_target="tpu_custom_call" | custom-call | flops 2147483648 | bytes 4194304 | tf_op jit(solution)/shard_map/attend/pallas_call | solution.py:108
  27.6 1.9 %collective-permute-start = (bf16[32,16,128]{2,1,0:T(8,128)(2,1)S(1)}, bf16[32,16,128]{2,1,0:T(8,128)(2,1)S(1)}, u32[]{:S(2)}, u32[]{:S(2)}) collective-permute-start(bf16[32,16,128]{2,1,0:T(8,128)(2,1)S(1)} %attend.1), channel_id=1, source_target_pairs={{0,32},{32,64},{64,96},{96,128},{128,160},{160,192},{192,224},{224... | collective-permute-start | bytes 393224 | tf_op jit(solution)/shard_map/ppermute | solution.py:152
  29.5 10.8 %collective-permute-done = bf16[32,16,128]{2,1,0:T(8,128)(2,1)S(1)} collective-permute-done((bf16[32,16,128]{2,1,0:T(8,128)(2,1)S(1)}, bf16[32,16,128]{2,1,0:T(8,128)(2,1)S(1)}, u32[]{:S(2)}, u32[]{:S(2)}) %collective-permute-start) | collective-permute-done | bytes 131104 | tf_op jit(solution)/shard_map/ppermute | solution.py:152
  40.4 11.5 %all_to_all.10 = bf16[32,16,128]{2,1,0:T(8,128)(2,1)S(1)} all-to-all(bf16[32,16,128]{2,1,0:T(8,128)(2,1)S(1)} %collective-permute-done), channel_id=1, replica_groups=mesh['section'=16,'seq'=32] {'seq'}, dimensions={0} | all-to-all | bytes 262144 | tf_op jit(solution)/shard_map/all_to_all | solution.py:153
  51.9 0.7 %copy_bitcast_fusion = bf16[1,16,4096]{2,1,0:T(8,128)(2,1)} fusion(bf16[32,16,128]{2,1,0:T(8,128)(2,1)S(1)} %all_to_all.10), kind=kLoop, calls=%fused_computation.3 | loop fusion | bytes 262144 | tf_op jit(solution)/shard_map/reshape | solution.py:155
Async XLA Ops:
  1.8 20.7 %all-to-all-start = ((bf16[32,48,128]{2,1,0:T(8,128)(2,1)}), bf16[32,48,128]{2,1,0:T(8,128)(2,1)S(1)}, u32[]{:S(2)}, u32[]{:S(2)}) async-start(bf16[32,48,128]{2,1,0:T(8,128)(2,1)} %bitcast.2), calls=%async_computation | async-start | bytes 786432 | tf_op jit(solution)/shard_map/all_to_all | solution.py:143
  27.6 12.8 %collective-permute-start = (bf16[32,16,128]{2,1,0:T(8,128)(2,1)S(1)}, bf16[32,16,128]{2,1,0:T(8,128)(2,1)S(1)}, u32[]{:S(2)}, u32[]{:S(2)}) collective-permute-start(bf16[32,16,128]{2,1,0:T(8,128)(2,1)S(1)} %attend.1), channel_id=1, source_target_pairs={{0,32},{32,64},{64,96},{96,128},{128,160},{160,192},{192,224},{224... | collective-permute-start | bytes 393224 | tf_op jit(solution)/shard_map/ppermute | solution.py:152

commit v4 on v3

--- a/solution.py
+++ b/solution.py
@@ -148,11 +148,11 @@
     back = pltpu.with_memory_space_constraint(back, pltpu.HBM)
     attended = attend(section_patch, qkv, keys, front, back)
 
+    handed = lax.all_to_all(attended, "seq", split_axis=0, concat_axis=0, tiled=True)
+    handed = handed.reshape(devices, tokens // 8, 8, width).transpose(1, 2, 0, 3)
+    handed = handed.reshape(1, tokens, total_width)
     pairs = [(source, (source + 1) % sections) for source in range(sections)]
-    handed = lax.ppermute(attended, "section", pairs)
-    handed = lax.all_to_all(handed, "seq", split_axis=0, concat_axis=0, tiled=True)
-    handed = handed.reshape(devices, tokens // 8, 8, width).transpose(1, 2, 0, 3)
-    return handed.reshape(1, tokens, total_width)
+    return lax.ppermute(handed, "section", pairs)
 
 
 def solution(mesh):

time: 52.9 us -> 52.5 us (level)
    unnamed x1 -> x2, local copies, waits for them, and re-layouts: 3.16 us -> 3.82 us
    reshape x1, local copies, waits for them, and re-layouts: 0.66 us -> 0.01 us  [body(): handed = handed.reshape(1, tokens, total_width)]
where the time goes in v4:
time: 52.5 us; the launch traced here: 52.2 us
  waiting for transfers between devices  16 us (30%)
  starting transfers between devices  12.3 us (23%)
  blocking collectives  11.2 us (21%)
  local copies, waits for them, and re-layouts  6.89 us (13%)
  Pallas kernels  5.07 us (10%)
  between operations  0.7 us (1%)
    all_to_all x1, blocking collectives, body(): lax.all_to_all(attended, 'seq', split_axis=0, concat_axis=0, tiled=True)  11.2 us
    ppermute x1, waiting for transfers between devices, body(): return lax.ppermute(handed, 'section', pairs)  10.8 us
    all_to_all x1, starting transfers between devices, body(): qkv = lax.all_to_all(packed, 'seq', split_axis=0, concat_axis=0, tiled=True)  10.4 us
    all_to_all x1, waiting for transfers between devices, body(): qkv = lax.all_to_all(packed, 'seq', split_axis=0, concat_axis=0, tiled=True)  5.21 us
    pallas_call x1, Pallas kernels, attend(): pl.pallas_call(functools.partial(attend_kernel, CHUNK), out_shape=jax.Sha...  5.07 us
    unnamed x2, local copies, waits for them, and re-layouts  3.82 us
    ppermute x1, starting transfers between devices, body(): return lax.ppermute(handed, 'section', pairs)  1.92 us
    another operation x1, local copies, waits for them, and re-layouts, body(): packed = fresh[0].reshape(tokens // 8, 8, parts, devices, width)  1.82 us
  transfers between devices with their start and end apart: 2, of which 2 were waited for; matrix products, arithmetic and copies ran while one was open for 8% of the time, Pallas kernels for 0%

profile of v4, /device:TPU:1, one launch (start us, length us, event | category | flops | bytes accessed | tf_op | source)
XLA Modules:
  0.0 52.2 jit_solution(620530794361956614)
XLA Ops:
  0.0 1.8 %copy.4 = bf16[2,8,3,32,128]{4,1,0,2,3:T(8,128)(2,1)} copy(bf16[2,8,3,32,128]{4,1,3,0,2:T(8,128)(2,1)} %bitcast.20) | data formatting | bytes 786432 | tf_op jit(solution)/shard_map/reshape;squeeze | solution.py:141
  1.8 10.4 %all-to-all-start = ((bf16[32,48,128]{2,1,0:T(8,128)(2,1)}), bf16[32,48,128]{2,1,0:T(8,128)(2,1)S(1)}, u32[]{:S(2)}, u32[]{:S(2)}) async-start(bf16[32,48,128]{2,1,0:T(8,128)(2,1)} %bitcast.2), calls=%async_computation | async-start | bytes 786432 | tf_op jit(solution)/shard_map/all_to_all | solution.py:143
  12.2 3.2 %copy.5 = bf16[1,16,512,2,128]{4,2,1,3,0:T(8,128)(2,1)S(1)} copy(bf16[1,16,512,2,128]{4,3,2,1,0:T(2,128)(2,1)} %param.4) | data formatting | bytes 8388608 | tf_op args[1]
  15.4 0.1 slice_bitcast_fusion.keys_ref
  15.6 1.1 %slice_bitcast_fusion.1 = (bf16[4096,128]{1,0:T(8,128)(2,1)}, bf16[4096,128]{1,0:T(8,128)(2,1)S(1)}) fusion(bf16[8192,2,128]{2,0,1:T(8,128)(2,1)S(1)} %bitcast.19), kind=kLoop, calls=%fused_computation.1 | loop fusion | bytes 4194304 | tf_op jit(solution)/shard_map/squeeze | solution.py:147
  17.3 5.2 %all-to-all-done.qkv_ref = bf16[32,48,128]{2,1,0:T(8,128)(2,1)S(1)} async-done(((bf16[32,48,128]{2,1,0:T(8,128)(2,1)}), bf16[32,48,128]{2,1,0:T(8,128)(2,1)S(1)}, u32[]{:S(2)}, u32[]{:S(2)}) %all-to-all-start) | async-done | bytes 393248 | tf_op jit(solution)/shard_map/all_to_all | solution.py:143
  22.5 5.1 %attend.1 = bf16[32,16,128]{2,1,0:T(8,128)(2,1)S(1)} custom-call(s32[1]{0:T(128)S(6)} %copy.9.own_ref, bf16[32,48,128]{2,1,0:T(8,128)(2,1)S(1)} %all-to-all-done.qkv_ref, bf16[8192,128]{1,0:T(8,128)(2,1)S(1)} %slice_bitcast_fusion.keys_ref, bf16[4096,128]{1,0:T(8,128)(2,1)S(1)} %get-tuple-element.6.front_ref, bf16[4096,128]{1,0:T(8,128)(2,1)} %get-tuple-element.5.back_hbm), custom_call_target="tpu_custom_call" | custom-call | flops 2147483648 | bytes 4194304 | tf_op jit(solution)/shard_map/attend/pallas_call | solution.py:108
  27.6 11.2 %all_to_all.10 = bf16[32,16,128]{2,1,0:T(8,128)(2,1)S(1)} all-to-all(bf16[32,16,128]{2,1,0:T(8,128)(2,1)S(1)} %attend.1), channel_id=1, replica_groups=mesh['section'=16,'seq'=32] {'seq'}, dimensions={0} | all-to-all | bytes 262144 | tf_op jit(solution)/shard_map/all_to_all | solution.py:151
  38.8 1.9 %collective-permute-start = (bf16[1,16,4096]{2,1,0:T(8,128)(2,1)S(1)}, bf16[1,16,4096]{2,1,0:T(8,128)(2,1)S(1)}, u32[]{:S(2)}, u32[]{:S(2)}) collective-permute-start(bf16[1,16,4096]{2,1,0:T(8,128)(2,1)S(1)} %copy_bitcast_fusion), channel_id=1, source_target_pairs={{0,32},{32,64},{64,96},{96,128},{128,160},{160,192},{192,224},{224... | collective-permute-start | bytes 393224 | tf_op jit(solution)/shard_map/ppermute | solution.py:155
  40.8 10.8 %collective-permute-done = bf16[1,16,4096]{2,1,0:T(8,128)(2,1)S(1)} collective-permute-done((bf16[1,16,4096]{2,1,0:T(8,128)(2,1)S(1)}, bf16[1,16,4096]{2,1,0:T(8,128)(2,1)S(1)}, u32[]{:S(2)}, u32[]{:S(2)}) %collective-permute-start) | collective-permute-done | bytes 131104 | tf_op jit(solution)/shard_map/ppermute | solution.py:155
  51.5 0.7 %copy.10 = bf16[1,16,4096]{2,1,0:T(8,128)(2,1)} copy(bf16[1,16,4096]{2,1,0:T(8,128)(2,1)S(1)} %collective-permute-done) | data formatting | bytes 262144
  (1 shorter events, 0.0 us)
Async XLA Ops:
  1.8 20.7 %all-to-all-start = ((bf16[32,48,128]{2,1,0:T(8,128)(2,1)}), bf16[32,48,128]{2,1,0:T(8,128)(2,1)S(1)}, u32[]{:S(2)}, u32[]{:S(2)}) async-start(bf16[32,48,128]{2,1,0:T(8,128)(2,1)} %bitcast.2), calls=%async_computation | async-start | bytes 786432 | tf_op jit(solution)/shard_map/all_to_all | solution.py:143
  38.8 12.7 %collective-permute-start = (bf16[1,16,4096]{2,1,0:T(8,128)(2,1)S(1)}, bf16[1,16,4096]{2,1,0:T(8,128)(2,1)S(1)}, u32[]{:S(2)}, u32[]{:S(2)}) collective-permute-start(bf16[1,16,4096]{2,1,0:T(8,128)(2,1)S(1)} %copy_bitcast_fusion), channel_id=1, source_target_pairs={{0,32},{32,64},{64,96},{96,128},{128,160},{160,192},{192,224},{224... | collective-permute-start | bytes 393224 | tf_op jit(solution)/shard_map/ppermute | solution.py:155

commit v5 on v4

--- a/solution.py
+++ b/solution.py
@@ -80,8 +80,9 @@
     summed = None
     later = []
     for index in range(count):
+        if index == 0:
+            later = [score(held + more) for more in range(held)]
         if index < held:
-            later.append(score(held + index))
             scores = scores_ref[index]
         else:
             scores = later[index - held]

time: 52.5 us -> 52.5 us (level)
  no operation moved by 1% of the time
where the time goes in v5:
time: 52.5 us; the launch traced here: 52.2 us
  waiting for transfers between devices  16 us (30%)
  starting transfers between devices  12.3 us (23%)
  blocking collectives  11.2 us (21%)
  local copies, waits for them, and re-layouts  6.89 us (13%)
  Pallas kernels  5.07 us (10%)
  between operations  0.7 us (1%)
    all_to_all x1, blocking collectives, body(): lax.all_to_all(attended, 'seq', split_axis=0, concat_axis=0, tiled=True)  11.2 us
    ppermute x1, waiting for transfers between devices, body(): return lax.ppermute(handed, 'section', pairs)  10.8 us
    all_to_all x1, starting transfers between devices, body(): qkv = lax.all_to_all(packed, 'seq', split_axis=0, concat_axis=0, tiled=True)  10.4 us
    all_to_all x1, waiting for transfers between devices, body(): qkv = lax.all_to_all(packed, 'seq', split_axis=0, concat_axis=0, tiled=True)  5.21 us
    pallas_call x1, Pallas kernels, attend(): pl.pallas_call(functools.partial(attend_kernel, CHUNK), out_shape=jax.Sha...  5.07 us
    unnamed x2, local copies, waits for them, and re-layouts  3.82 us
    ppermute x1, starting transfers between devices, body(): return lax.ppermute(handed, 'section', pairs)  1.92 us
    another operation x1, local copies, waits for them, and re-layouts, body(): packed = fresh[0].reshape(tokens // 8, 8, parts, devices, width)  1.82 us
  transfers between devices with their start and end apart: 2, of which 2 were waited for; matrix products, arithmetic and copies ran while one was open for 8% of the time, Pallas kernels for 0%

profile of v5, /device:TPU:1, one launch (start us, length us, event | category | flops | bytes accessed | tf_op | source)
XLA Modules:
  0.0 52.2 jit_solution(620530794361956614)
XLA Ops:
  0.0 1.8 %copy.4 = bf16[2,8,3,32,128]{4,1,0,2,3:T(8,128)(2,1)} copy(bf16[2,8,3,32,128]{4,1,3,0,2:T(8,128)(2,1)} %bitcast.20) | data formatting | bytes 786432 | tf_op jit(solution)/shard_map/reshape;squeeze | solution.py:142
  1.8 10.4 %all-to-all-start = ((bf16[32,48,128]{2,1,0:T(8,128)(2,1)}), bf16[32,48,128]{2,1,0:T(8,128)(2,1)S(1)}, u32[]{:S(2)}, u32[]{:S(2)}) async-start(bf16[32,48,128]{2,1,0:T(8,128)(2,1)} %bitcast.2), calls=%async_computation | async-start | bytes 786432 | tf_op jit(solution)/shard_map/all_to_all | solution.py:144
  12.2 3.2 %copy.5 = bf16[1,16,512,2,128]{4,2,1,3,0:T(8,128)(2,1)S(1)} copy(bf16[1,16,512,2,128]{4,3,2,1,0:T(2,128)(2,1)} %param.4) | data formatting | bytes 8388608 | tf_op args[1]
  15.4 0.1 slice_bitcast_fusion.keys_ref
  15.6 1.1 %slice_bitcast_fusion.1 = (bf16[4096,128]{1,0:T(8,128)(2,1)}, bf16[4096,128]{1,0:T(8,128)(2,1)S(1)}) fusion(bf16[8192,2,128]{2,0,1:T(8,128)(2,1)S(1)} %bitcast.19), kind=kLoop, calls=%fused_computation.1 | loop fusion | bytes 4194304 | tf_op jit(solution)/shard_map/squeeze | solution.py:148
  17.3 5.2 %all-to-all-done.qkv_ref = bf16[32,48,128]{2,1,0:T(8,128)(2,1)S(1)} async-done(((bf16[32,48,128]{2,1,0:T(8,128)(2,1)}), bf16[32,48,128]{2,1,0:T(8,128)(2,1)S(1)}, u32[]{:S(2)}, u32[]{:S(2)}) %all-to-all-start) | async-done | bytes 393248 | tf_op jit(solution)/shard_map/all_to_all | solution.py:144
  22.5 5.1 %attend.1 = bf16[32,16,128]{2,1,0:T(8,128)(2,1)S(1)} custom-call(s32[1]{0:T(128)S(6)} %copy.9.own_ref, bf16[32,48,128]{2,1,0:T(8,128)(2,1)S(1)} %all-to-all-done.qkv_ref, bf16[8192,128]{1,0:T(8,128)(2,1)S(1)} %slice_bitcast_fusion.keys_ref, bf16[4096,128]{1,0:T(8,128)(2,1)S(1)} %get-tuple-element.6.front_ref, bf16[4096,128]{1,0:T(8,128)(2,1)} %get-tuple-element.5.back_hbm), custom_call_target="tpu_custom_call" | custom-call | flops 2147483648 | bytes 4194304 | tf_op jit(solution)/shard_map/attend/pallas_call | solution.py:109
  27.6 11.2 %all_to_all.10 = bf16[32,16,128]{2,1,0:T(8,128)(2,1)S(1)} all-to-all(bf16[32,16,128]{2,1,0:T(8,128)(2,1)S(1)} %attend.1), channel_id=1, replica_groups=mesh['section'=16,'seq'=32] {'seq'}, dimensions={0} | all-to-all | bytes 262144 | tf_op jit(solution)/shard_map/all_to_all | solution.py:152
  38.8 1.9 %collective-permute-start = (bf16[1,16,4096]{2,1,0:T(8,128)(2,1)S(1)}, bf16[1,16,4096]{2,1,0:T(8,128)(2,1)S(1)}, u32[]{:S(2)}, u32[]{:S(2)}) collective-permute-start(bf16[1,16,4096]{2,1,0:T(8,128)(2,1)S(1)} %copy_bitcast_fusion), channel_id=1, source_target_pairs={{0,32},{32,64},{64,96},{96,128},{128,160},{160,192},{192,224},{224... | collective-permute-start | bytes 393224 | tf_op jit(solution)/shard_map/ppermute | solution.py:156
  40.8 10.8 %collective-permute-done = bf16[1,16,4096]{2,1,0:T(8,128)(2,1)S(1)} collective-permute-done((bf16[1,16,4096]{2,1,0:T(8,128)(2,1)S(1)}, bf16[1,16,4096]{2,1,0:T(8,128)(2,1)S(1)}, u32[]{:S(2)}, u32[]{:S(2)}) %collective-permute-start) | collective-permute-done | bytes 131104 | tf_op jit(solution)/shard_map/ppermute | solution.py:156
  51.5 0.7 %copy.10 = bf16[1,16,4096]{2,1,0:T(8,128)(2,1)} copy(bf16[1,16,4096]{2,1,0:T(8,128)(2,1)S(1)} %collective-permute-done) | data formatting | bytes 262144
  (1 shorter events, 0.0 us)
Async XLA Ops:
  1.8 20.7 %all-to-all-start = ((bf16[32,48,128]{2,1,0:T(8,128)(2,1)}), bf16[32,48,128]{2,1,0:T(8,128)(2,1)S(1)}, u32[]{:S(2)}, u32[]{:S(2)}) async-start(bf16[32,48,128]{2,1,0:T(8,128)(2,1)} %bitcast.2), calls=%async_computation | async-start | bytes 786432 | tf_op jit(solution)/shard_map/all_to_all | solution.py:144
  38.8 12.7 %collective-permute-start = (bf16[1,16,4096]{2,1,0:T(8,128)(2,1)S(1)}, bf16[1,16,4096]{2,1,0:T(8,128)(2,1)S(1)}, u32[]{:S(2)}, u32[]{:S(2)}) collective-permute-start(bf16[1,16,4096]{2,1,0:T(8,128)(2,1)S(1)} %copy_bitcast_fusion), channel_id=1, source_target_pairs={{0,32},{32,64},{64,96},{96,128},{128,160},{160,192},{192,224},{224... | collective-permute-start | bytes 393224 | tf_op jit(solution)/shard_map/ppermute | solution.py:156

commit v6 on v5

--- a/solution.py
+++ b/solution.py
@@ -150,10 +150,10 @@
     attended = attend(section_patch, qkv, keys, front, back)
 
     handed = lax.all_to_all(attended, "seq", split_axis=0, concat_axis=0, tiled=True)
+    pairs = [(source, (source + 1) % sections) for source in range(sections)]
+    handed = lax.ppermute(handed, "section", pairs)
     handed = handed.reshape(devices, tokens // 8, 8, width).transpose(1, 2, 0, 3)
-    handed = handed.reshape(1, tokens, total_width)
-    pairs = [(source, (source + 1) % sections) for source in range(sections)]
-    return lax.ppermute(handed, "section", pairs)
+    return handed.reshape(1, tokens, total_width)
 
 
 def solution(mesh):

time: 52.5 us -> 52.5 us (level)
    unnamed x2 -> x1, local copies, waits for them, and re-layouts: 3.82 us -> 3.16 us
    reshape x1, local copies, waits for them, and re-layouts: 0.01 us -> 0.66 us  [body(): return handed.reshape(1, tokens, total_width)]
where the time goes in v6:
time: 52.5 us; the launch traced here: 52.2 us
  waiting for transfers between devices  16 us (30%)
  starting transfers between devices  12.3 us (23%)
  blocking collectives  11.2 us (21%)
  local copies, waits for them, and re-layouts  6.89 us (13%)
  Pallas kernels  5.05 us (10%)
  between operations  0.69 us (1%)
    all_to_all x1, blocking collectives, body(): lax.all_to_all(attended, 'seq', split_axis=0, concat_axis=0, tiled=True)  11.2 us
    ppermute x1, waiting for transfers between devices, body(): handed = lax.ppermute(handed, 'section', pairs)  10.8 us
    all_to_all x1, starting transfers between devices, body(): qkv = lax.all_to_all(packed, 'seq', split_axis=0, concat_axis=0, tiled=True)  10.4 us
    all_to_all x1, waiting for transfers between devices, body(): qkv = lax.all_to_all(packed, 'seq', split_axis=0, concat_axis=0, tiled=True)  5.21 us
    pallas_call x1, Pallas kernels, attend(): pl.pallas_call(functools.partial(attend_kernel, CHUNK), out_shape=jax.Sha...  5.05 us
    unnamed x1, local copies, waits for them, and re-layouts  3.16 us
    ppermute x1, starting transfers between devices, body(): handed = lax.ppermute(handed, 'section', pairs)  1.91 us
    another operation x1, local copies, waits for them, and re-layouts, body(): packed = fresh[0].reshape(tokens // 8, 8, parts, devices, width)  1.82 us
  transfers between devices with their start and end apart: 2, of which 2 were waited for; matrix products, arithmetic and copies ran while one was open for 8% of the time, Pallas kernels for 0%

profile of v6, /device:TPU:1, one launch (start us, length us, event | category | flops | bytes accessed | tf_op | source)
XLA Modules:
  0.0 52.2 jit_solution(2684757769115052589)
XLA Ops:
  0.0 1.8 %copy.4 = bf16[2,8,3,32,128]{4,1,0,2,3:T(8,128)(2,1)} copy(bf16[2,8,3,32,128]{4,1,3,0,2:T(8,128)(2,1)} %bitcast.20) | data formatting | bytes 786432 | tf_op jit(solution)/shard_map/reshape;squeeze | solution.py:142
  1.8 10.4 %all-to-all-start = ((bf16[32,48,128]{2,1,0:T(8,128)(2,1)}), bf16[32,48,128]{2,1,0:T(8,128)(2,1)S(1)}, u32[]{:S(2)}, u32[]{:S(2)}) async-start(bf16[32,48,128]{2,1,0:T(8,128)(2,1)} %bitcast.2), calls=%async_computation | async-start | bytes 786432 | tf_op jit(solution)/shard_map/all_to_all | solution.py:144
  12.2 3.2 %copy.5 = bf16[1,16,512,2,128]{4,2,1,3,0:T(8,128)(2,1)S(1)} copy(bf16[1,16,512,2,128]{4,3,2,1,0:T(2,128)(2,1)} %param.4) | data formatting | bytes 8388608 | tf_op args[1]
  15.4 0.1 slice_bitcast_fusion.keys_ref
  15.6 1.1 %slice_bitcast_fusion.1 = (bf16[4096,128]{1,0:T(8,128)(2,1)}, bf16[4096,128]{1,0:T(8,128)(2,1)S(1)}) fusion(bf16[8192,2,128]{2,0,1:T(8,128)(2,1)S(1)} %bitcast.19), kind=kLoop, calls=%fused_computation.1 | loop fusion | bytes 4194304 | tf_op jit(solution)/shard_map/squeeze | solution.py:148
  17.3 5.2 %all-to-all-done.qkv_ref = bf16[32,48,128]{2,1,0:T(8,128)(2,1)S(1)} async-done(((bf16[32,48,128]{2,1,0:T(8,128)(2,1)}), bf16[32,48,128]{2,1,0:T(8,128)(2,1)S(1)}, u32[]{:S(2)}, u32[]{:S(2)}) %all-to-all-start) | async-done | bytes 393248 | tf_op jit(solution)/shard_map/all_to_all | solution.py:144
  22.5 5.1 %attend.1 = bf16[32,16,128]{2,1,0:T(8,128)(2,1)S(1)} custom-call(s32[1]{0:T(128)S(6)} %copy.8.own_ref, bf16[32,48,128]{2,1,0:T(8,128)(2,1)S(1)} %all-to-all-done.qkv_ref, bf16[8192,128]{1,0:T(8,128)(2,1)S(1)} %slice_bitcast_fusion.keys_ref, bf16[4096,128]{1,0:T(8,128)(2,1)S(1)} %get-tuple-element.6.front_ref, bf16[4096,128]{1,0:T(8,128)(2,1)} %get-tuple-element.5.back_hbm), custom_call_target="tpu_custom_call" | custom-call | flops 2147483648 | bytes 4194304 | tf_op jit(solution)/shard_map/attend/pallas_call | solution.py:109
  27.6 11.2 %all_to_all.10 = bf16[32,16,128]{2,1,0:T(8,128)(2,1)S(1)} all-to-all(bf16[32,16,128]{2,1,0:T(8,128)(2,1)S(1)} %attend.1), channel_id=1, replica_groups=mesh['section'=16,'seq'=32] {'seq'}, dimensions={0} | all-to-all | bytes 262144 | tf_op jit(solution)/shard_map/all_to_all | solution.py:152
  38.8 1.9 %collective-permute-start = (bf16[32,16,128]{2,1,0:T(8,128)(2,1)S(1)}, bf16[32,16,128]{2,1,0:T(8,128)(2,1)S(1)}, u32[]{:S(2)}, u32[]{:S(2)}) collective-permute-start(bf16[32,16,128]{2,1,0:T(8,128)(2,1)S(1)} %all_to_all.10), channel_id=1, source_target_pairs={{0,32},{32,64},{64,96},{96,128},{128,160},{160,192},{192,224},{224... | collective-permute-start | bytes 393224 | tf_op jit(solution)/shard_map/ppermute | solution.py:154
  40.7 10.8 %collective-permute-done = bf16[32,16,128]{2,1,0:T(8,128)(2,1)S(1)} collective-permute-done((bf16[32,16,128]{2,1,0:T(8,128)(2,1)S(1)}, bf16[32,16,128]{2,1,0:T(8,128)(2,1)S(1)}, u32[]{:S(2)}, u32[]{:S(2)}) %collective-permute-start) | collective-permute-done | bytes 131104 | tf_op jit(solution)/shard_map/ppermute | solution.py:154
  51.5 0.7 %copy_bitcast_fusion = bf16[1,16,4096]{2,1,0:T(8,128)(2,1)} fusion(bf16[32,16,128]{2,1,0:T(8,128)(2,1)S(1)} %collective-permute-done), kind=kLoop, calls=%fused_computation.3 | loop fusion | bytes 262144 | tf_op jit(solution)/shard_map/reshape | solution.py:156
Async XLA Ops:
  1.8 20.7 %all-to-all-start = ((bf16[32,48,128]{2,1,0:T(8,128)(2,1)}), bf16[32,48,128]{2,1,0:T(8,128)(2,1)S(1)}, u32[]{:S(2)}, u32[]{:S(2)}) async-start(bf16[32,48,128]{2,1,0:T(8,128)(2,1)} %bitcast.2), calls=%async_computation | async-start | bytes 786432 | tf_op jit(solution)/shard_map/all_to_all | solution.py:144
  38.8 12.7 %collective-permute-start = (bf16[32,16,128]{2,1,0:T(8,128)(2,1)S(1)}, bf16[32,16,128]{2,1,0:T(8,128)(2,1)S(1)}, u32[]{:S(2)}, u32[]{:S(2)}) collective-permute-start(bf16[32,16,128]{2,1,0:T(8,128)(2,1)S(1)} %all_to_all.10), channel_id=1, source_target_pairs={{0,32},{32,64},{64,96},{96,128},{128,160},{160,192},{192,224},{224... | collective-permute-start | bytes 393224 | tf_op jit(solution)/shard_map/ppermute | solution.py:154
